TPU v7x, 1024 devices: a whole 8x8x8 slice. The times are simulated.
1024 devices in a mesh: blk: 32 (over x, y_hi), grp: 32 (over z, y_lo, core).
Axes of the slice: x: 8, y: 8 (y_hi: 4, y_lo: 2; y = y_hi * 2 + y_lo), z: 8, core: 2. Of those that a mesh axis runs over, the one named last changes fastest.
Arguments:
- image: bfloat16 [262144, 1152], P(('blk', 'grp')), may hold values from -0.1875 to 0.1875
- text: bfloat16 [262144, 1152], P(('blk', 'grp')), may hold values from -0.1875 to 0.1875
- log_temp: float32 [1], replicated, may hold values from 1.6 to 3
- bias: float32 [1], replicated, may hold values from -4 to -1
Outputs:
- grad_image: float32 [262144, 1152], P(('blk', 'grp'))
- grad_text: float32 [262144, 1152], P(('blk', 'grp'))
- grad_log_temp: float32 [1], replicated
- grad_bias: float32 [1], replicated
All inputs are finite; a program needn't handle non-finite values.
Results may differ from a plain program's by a relative error of at most 0.0024.
Values may be sent and summed in bfloat16 or wider, within the bound.
A program may use at most 32 MiB of HBM per device.

v0:
```python
import jax
import jax.numpy as jnp
from jax import lax
from jax.sharding import PartitionSpec as P


def passed_along(value, axis, steps):
    count = lax.axis_size(axis)
    pairs = [(source, (source + steps) % count) for source in range(count)]
    return lax.ppermute(value, axis, pairs)


def unit_rows(rows_in):
    values = rows_in.astype(jnp.float32)
    length = jnp.sqrt(jnp.sum(values * values, axis=-1, keepdims=True) + 1e-06)
    return (values / length, length)


def norm_back(unit, length, grad_unit):
    inner = jnp.sum(unit * grad_unit, axis=-1, keepdims=True)
    return (grad_unit - unit * inner) / length


def pair_dot(left, right):
    return lax.dot_general(
        left, right, (((1,), (1,)), ((), ())), preferred_element_type=jnp.float32
    )


def first_dot(left, right):
    return lax.dot_general(
        left, right, (((0,), (0,)), ((), ())), preferred_element_type=jnp.float32
    )


def local(image, text, log_temp, bias):
    temp = jnp.exp(log_temp[0])
    shift_b = bias[0]
    count = image.shape[0]
    img_unit, img_len = unit_rows(image)
    txt_unit, txt_len = unit_rows(text)
    img_half = img_unit.astype(jnp.bfloat16)
    txt_half = txt_unit.astype(jnp.bfloat16)
    prev_half = passed_along(txt_half, "blk", 1)
    rows = lax.broadcasted_iota(jnp.int32, (count, count), 0)
    cols = lax.broadcasted_iota(jnp.int32, (count, count), 1)
    sign = jnp.where(rows == cols, 1.0, -1.0).astype(jnp.float32)
    own = temp * pair_dot(img_half, txt_half) + shift_b
    near = temp * pair_dot(img_half, prev_half) + shift_b
    coef_own = -sign * jax.nn.sigmoid(-sign * own)
    coef_near = jax.nn.sigmoid(near)
    half_own = coef_own.astype(jnp.bfloat16)
    half_near = coef_near.astype(jnp.bfloat16)
    d_img = temp * (
        jnp.dot(half_own, txt_half, preferred_element_type=jnp.float32)
        + jnp.dot(half_near, prev_half, preferred_element_type=jnp.float32)
    )
    own_txt = temp * first_dot(half_own, img_half)
    outgoing = temp * first_dot(half_near, img_half)
    d_txt = own_txt + passed_along(outgoing, "blk", -1)
    sum_c = jnp.sum(coef_own) + jnp.sum(coef_near)
    sum_cl = jnp.sum(coef_own * (own - shift_b)) + jnp.sum(coef_near * (near - shift_b))
    total_c, total_cl = lax.psum((sum_c, sum_cl), ("blk", "grp"))
    scale = jnp.float32(count * lax.axis_size("blk") * lax.axis_size("grp"))
    grad_image = norm_back(img_unit, img_len, d_img)
    grad_text = norm_back(txt_unit, txt_len, d_txt)
    return (grad_image, grad_text, (total_cl / scale).reshape(1), (total_c / scale).reshape(1))


def solution(mesh):
    in_specs = (P(("blk", "grp"), None), P(("blk", "grp"), None), P(), P())
    out_specs = (P(("blk", "grp"), None), P(("blk", "grp"), None), P(), P())
    return jax.shard_map(local, mesh=mesh, in_specs=in_specs, out_specs=out_specs, check_vma=False)
```

profile of v0, /device:TPU:1, one launch (start us, length us, event | category | flops | bytes accessed | tf_op | source)
XLA Modules:
  0.0 220.8 jit_solution(8266195893740244621)
XLA Ops:
  0.6 0.0 copy-start.1
  0.6 1.3 fusion.3
  2.0 1.3 fusion.12
  3.3 5.3 %collective-permute-start = (bf16[256,1152]{1,0:T(8,128)(2,1)S(1)}, bf16[256,1152]{1,0:T(8,128)(2,1)S(1)}, u32[]{:S(2)}, u32[]{:S(2)}) collective-permute-start(bf16[256,1152]{1,0:T(8,128)(2,1)S(1)} %fusion.12), channel_id=1, source_target_pairs={{0,32},{32,64},{64,96},{96,128},{128,160},{160,192},{192,224},{224... | collective-permute-start | bytes 1769480 | tf_op jit(solution)/shard_map/ppermute | solution.py:10
  8.5 0.0 copy-done.1
  8.6 0.2 fusion.2
  10.1 1.1 fusion.14
  11.2 15.7 %collective-permute-done = bf16[256,1152]{1,0:T(8,128)(2,1)S(1)} collective-permute-done((bf16[256,1152]{1,0:T(8,128)(2,1)S(1)}, bf16[256,1152]{1,0:T(8,128)(2,1)S(1)}, u32[]{:S(2)}, u32[]{:S(2)}) %collective-permute-start) | collective-permute-done | bytes 589856 | tf_op jit(solution)/shard_map/ppermute | solution.py:10
  26.9 1.1 fusion.13
  27.9 1.4 convolution_multiply_fusion
  29.4 12.5 %collective-permute-start.1 = (f32[256,1152]{1,0:T(8,128)}, f32[256,1152]{1,0:T(8,128)}, u32[]{:S(2)}, u32[]{:S(2)}) collective-permute-start(f32[256,1152]{1,0:T(8,128)} %convolution_multiply_fusion), channel_id=1, source_target_pairs={{0,992},{32,0},{64,32},{96,64},{128,96},{160,128},{192,160},{224,1... | collective-permute-start | bytes 3538952 | tf_op jit(solution)/shard_map/ppermute | solution.py:10
  44.4 0.4 fusion.9
  44.7 167.5 %all-reduce = (f32[]{:T(128)}, f32[]{:T(128)}) all-reduce(f32[]{:T(128)S(6)} %add.57, f32[]{:T(128)S(6)} %add.58), channel_id=1, replica_groups=mesh['blk'=32,'grp'=32] {'blk','grp'}, use_global_device_ids=true, to_apply=%region_6.7 | all-reduce | flops 2 | bytes 16 | tf_op jit(solution)/shard_map/psum | solution.py:63
  213.6 0.5 multiply_reduce_fusion.1
  214.1 0.0 copy-start
  214.1 1.3 subtract_divide_fusion.1
  215.4 0.0 collective-permute-done.1
  215.4 0.0 copy-done
  215.4 1.8 multiply_reduce_fusion
  217.2 1.3 subtract_divide_fusion
  (2 shorter events, 0.0 us)
Async XLA Ops:
  0.6 7.9 %copy-start.1 = (bf16[256,1152]{1,0:T(8,128)(2,1)S(1)}, bf16[256,1152]{1,0:T(8,128)(2,1)}, u32[]{:S(2)}) copy-start(bf16[256,1152]{1,0:T(8,128)(2,1)} %param.4) | copy-start | bytes 1769476
  3.3 23.6 %collective-permute-start = (bf16[256,1152]{1,0:T(8,128)(2,1)S(1)}, bf16[256,1152]{1,0:T(8,128)(2,1)S(1)}, u32[]{:S(2)}, u32[]{:S(2)}) collective-permute-start(bf16[256,1152]{1,0:T(8,128)(2,1)S(1)} %fusion.12), channel_id=1, source_target_pairs={{0,32},{32,64},{64,96},{96,128},{128,160},{160,192},{192,224},{224... | collective-permute-start | bytes 1769480 | tf_op jit(solution)/shard_map/ppermute | solution.py:10
  29.4 186.0 %collective-permute-start.1 = (f32[256,1152]{1,0:T(8,128)}, f32[256,1152]{1,0:T(8,128)}, u32[]{:S(2)}, u32[]{:S(2)}) collective-permute-start(f32[256,1152]{1,0:T(8,128)} %convolution_multiply_fusion), channel_id=1, source_target_pairs={{0,992},{32,0},{64,32},{96,64},{128,96},{160,128},{192,160},{224,1... | collective-permute-start | bytes 3538952 | tf_op jit(solution)/shard_map/ppermute | solution.py:10
  214.1 1.3 copy-start
where the time goes:
time: 221 us
  blocking collectives  168 us (76%)
  starting transfers between devices  17.7 us (8%)
  waiting for transfers between devices  15.7 us (7%)
  between operations  8.11 us (4%)
  matrix products  6.27 us (3%)
  other arithmetic  5.4 us (2%)
    psum x1, blocking collectives, local(): total_c, total_cl = lax.psum((sum_c, sum_cl), ('blk', 'grp'))  168 us
    ppermute x2, starting transfers between devices, passed_along(): return lax.ppermute(value, axis, pairs)  17.7 us
    ppermute x2, waiting for transfers between devices, passed_along(): return lax.ppermute(value, axis, pairs)  15.7 us
  transfers between devices with their start and end apart: 2, of which 1 were waited for; matrix products, arithmetic and copies ran while one was open for 2% of the time, Pallas kernels for 0%

commit v1 on v0

v1 whole, which is shorter than its diff:
```python
import functools

import jax
import jax.numpy as jnp
from jax import lax
from jax.experimental import pallas as pl
from jax.experimental.pallas import tpu as pltpu
from jax.sharding import PartitionSpec as P

MESH = pl.DeviceIdType.MESH
Y_HI, Y_LO, CORES = 4, 2, 2
CHUNKS = 8
HOLD = 5


def row_dot(left, right):
    return lax.dot_general(
        left, right, (((1,), (1,)), ((), ())), preferred_element_type=jnp.float32
    )


def plain_dot(left, right):
    return lax.dot_general(
        left, right, (((1,), (0,)), ((), ())), preferred_element_type=jnp.float32
    )


def fold(tile):
    rows, cols = tile.shape
    part = jnp.sum(tile.reshape(rows // 8, 8, cols), axis=0)
    return functools.reduce(
        jnp.add, [part[:, at : at + 128] for at in range(0, cols, 128)]
    )


def kernel(
    sizes, img_in, txt_in, log_temp, bias, gi_out, gt_out, cl_out, c_out,
    img_raw, txt_raw, img_half, txt_half, img_inv, txt_inv,
    mid_txt, mid_img, end_txt, end_img, acc_txt, acc_img, sums,
    part, load_sem, send_sem, recv_sem, sum_send, sum_recv,
):
    blk_n, grp_n, total_pairs = sizes
    x_n, z_n = blk_n // Y_HI, grp_n // (Y_LO * CORES)
    rows = img_raw.shape[0]
    step = rows // CHUNKS

    me, grp = lax.axis_index("blk"), lax.axis_index("grp")
    x, y_hi = lax.div(me, Y_HI), lax.rem(me, Y_HI)
    z, low = lax.div(grp, Y_LO * CORES), lax.rem(grp, Y_LO * CORES)
    y_lo, core = lax.div(low, CORES), lax.rem(low, CORES)
    y = y_hi * Y_LO + y_lo

    def at(x, y, z, core):
        return (
            x * Y_HI + lax.div(y, Y_LO),
            z * (Y_LO * CORES) + lax.rem(y, Y_LO) * CORES + core,
        )

    other = z * (Y_LO * CORES) + (1 - y_lo) * CORES + core
    before = lax.rem(me + blk_n - 1, blk_n)
    meet_next = (x * Y_HI + lax.rem(y_hi + y_lo, Y_HI), other)
    meet_prev = (
        lax.div(before, Y_HI) * Y_HI + lax.rem(lax.rem(before, Y_HI) + y_lo, Y_HI),
        other,
    )
    first_blk = x * Y_HI + lax.rem(y_hi + y_lo + Y_HI - 1, Y_HI)
    first = (first_blk, other)
    second = (lax.rem(first_blk + 1, blk_n), other)

    levels = (
        (CORES, core, lambda k: at(x, y, z, k)),
        (z_n, z, lambda k: at(x, y, k, core)),
        (x_n, x, lambda k: at(k, y, z, core)),
        (Y_HI * Y_LO, y, lambda k: at(x, k, z, core)),
    )

    loads = [
        pltpu.make_async_copy(img_in, img_raw, load_sem.at[0]),
        pltpu.make_async_copy(txt_in, txt_raw, load_sem.at[1]),
    ]
    for load in loads:
        load.start()

    barrier = pltpu.get_barrier_semaphore()
    greeted = 0
    for device in (meet_next, meet_prev, first, second):
        pl.semaphore_signal(barrier, inc=1, device_id=device, device_id_type=MESH)
        greeted += 1
    for count, mine, place in levels:
        for k in range(1, count):
            pl.semaphore_signal(
                barrier, inc=1, device_id=place(lax.rem(mine + k, count)),
                device_id_type=MESH,
            )
            greeted += 1

    temp = jnp.exp(jnp.full((1, 1), log_temp[0], jnp.float32))
    shift = bias[0]

    def window(c):
        return pl.ds(c * step, step)

    def remote(src, dst, kind, c, device):
        return pltpu.make_async_remote_copy(
            src_ref=src.at[window(c), :],
            dst_ref=dst.at[window(c), :],
            send_sem=send_sem.at[kind, c],
            recv_sem=recv_sem.at[kind, c],
            device_id=device,
            device_id_type=MESH,
        )

    def normalize(raw, half, inv, c):
        values = raw[window(c), :].astype(jnp.float32)
        scale = 1.0 / jnp.sqrt(jnp.sum(values * values, axis=-1, keepdims=True) + 1e-06)
        inv[window(c), :] = scale
        half[window(c), :] = (values * scale).astype(jnp.bfloat16)

    for load in loads:
        load.wait()
    for c in range(CHUNKS):
        normalize(txt_raw, txt_half, txt_inv, c)
        normalize(img_raw, img_half, img_inv, c)
        if c == 0:
            pl.semaphore_wait(barrier, greeted)
        remote(txt_half, mid_txt, 0, c, meet_next).start()
        remote(img_half, mid_img, 1, c, meet_prev).start()

    def coefs(sims, diagonal):
        scaled = temp * sims
        logit = scaled + shift
        if not diagonal:
            return jax.nn.sigmoid(logit), scaled
        row = lax.broadcasted_iota(jnp.int32, sims.shape, 0)
        col = lax.broadcasted_iota(jnp.int32, sims.shape, 1)
        paired = row == col
        coef = jax.nn.sigmoid(jnp.where(paired, -logit, logit))
        return jnp.where(paired, -coef, coef), scaled

    coef, scaled = coefs(row_dot(img_half[...], txt_half[...]), True)
    own_c, own_cl = fold(coef), fold(coef * scaled)
    half = coef.astype(jnp.bfloat16)
    acc_img[...] = plain_dot(half, txt_half[...])
    half = coef.T.astype(jnp.bfloat16)
    acc_txt[...] = plain_dot(half, img_half[...])

    def arrived(c):
        remote(txt_half, mid_txt, 0, c, meet_next).wait_recv()
        remote(img_half, mid_img, 1, c, meet_prev).wait_recv()

    def send_on(c):
        remote(mid_txt, end_txt, 2, c, second).start()
        remote(mid_img, end_img, 3, c, first).start()

    for c in range(HOLD):
        arrived(c)
    for c in range(HOLD):
        send_on(c)
    for c in range(HOLD, CHUNKS):
        arrived(c)
        send_on(c)

    coef, scaled = coefs(row_dot(mid_img[...], mid_txt[...]), False)
    part[0:8, :] = own_c + fold(coef)
    part[8:16, :] = own_cl + fold(coef * scaled)
    tile = jnp.concatenate(
        [
            jnp.sum(part[0:8, :], axis=0, keepdims=True),
            jnp.sum(part[8:16, :], axis=0, keepdims=True),
            jnp.zeros((6, 128), jnp.float32),
        ],
        axis=0,
    )

    def exchange(level, mine, place, k, count):
        return pltpu.make_async_remote_copy(
            src_ref=sums.at[level, mine],
            dst_ref=sums.at[level, mine],
            send_sem=sum_send.at[level, k],
            recv_sem=sum_recv.at[level, mine],
            device_id=place(lax.rem(mine + k, count)),
            device_id_type=MESH,
        )

    for level, (count, mine, place) in enumerate(levels):
        sums[level, mine] = tile
        for k in range(1, count):
            exchange(level, mine, place, k, count).start()
        for k in range(1, count):
            source = lax.rem(mine + k, count)
            pltpu.make_async_remote_copy(
                src_ref=sums.at[level, source],
                dst_ref=sums.at[level, source],
                send_sem=sum_send.at[level, k],
                recv_sem=sum_recv.at[level, source],
                device_id=place(source),
                device_id_type=MESH,
            ).wait_recv()
        tile = sums[level, 0]
        for k in range(1, count):
            tile = tile + sums[level, k]
    c_out[0] = jnp.sum(tile[0:1, :]) / total_pairs
    cl_out[0] = jnp.sum(tile[1:2, :]) / total_pairs

    def finish(raw, half, inv, acc, visitors, out):
        coef, _ = coefs(row_dot(half[...], visitors[...]), False)
        grad = temp * (acc[...] + plain_dot(coef.astype(jnp.bfloat16), visitors[...]))
        scale = inv[...]
        unit = raw[...].astype(jnp.float32) * scale
        inner = jnp.sum(unit * grad, axis=-1, keepdims=True)
        out[...] = (grad - unit * inner) * scale

    for c in range(CHUNKS):
        remote(mid_txt, end_txt, 2, c, second).wait_recv()
    finish(img_raw, img_half, img_inv, acc_img, end_txt, gi_out)
    for c in range(CHUNKS):
        remote(mid_img, end_img, 3, c, first).wait_recv()
    finish(txt_raw, txt_half, txt_inv, acc_txt, end_img, gt_out)

    for c in range(CHUNKS):
        remote(txt_half, mid_txt, 0, c, meet_next).wait_send()
        remote(img_half, mid_img, 1, c, meet_prev).wait_send()
        remote(mid_txt, end_txt, 2, c, second).wait_send()
        remote(mid_img, end_img, 3, c, first).wait_send()
    for level, (count, mine, place) in enumerate(levels):
        for k in range(1, count):
            exchange(level, mine, place, k, count).wait_send()


def local(blk_n, grp_n, image, text, log_temp, bias):
    rows, width = image.shape
    most = max(CORES, grp_n // (Y_LO * CORES), blk_n // Y_HI, Y_HI * Y_LO)
    wide = jax.ShapeDtypeStruct((rows, width), jnp.float32)
    one = jax.ShapeDtypeStruct((1,), jnp.float32)
    half = pltpu.VMEM((rows, width), jnp.bfloat16)
    full = pltpu.VMEM((rows, width), jnp.float32)
    thin = pltpu.VMEM((rows, 1), jnp.float32)
    vmem, smem = pl.BlockSpec(memory_space=pltpu.VMEM), pl.BlockSpec(memory_space=pltpu.SMEM)
    hbm = pl.BlockSpec(memory_space=pl.ANY)
    dma = pltpu.SemaphoreType.DMA
    grad_image, grad_text, total_cl, total_c = pl.pallas_call(
        functools.partial(kernel, (blk_n, grp_n, float(rows * blk_n * grp_n))),
        out_shape=(wide, wide, one, one),
        in_specs=[hbm, hbm, smem, smem],
        out_specs=(vmem, vmem, smem, smem),
        scratch_shapes=[
            half, half, half, half, thin, thin,
            half, half, half, half, full, full,
            pltpu.VMEM((4, most, 8, 128), jnp.float32),
            pltpu.VMEM((16, 128), jnp.float32),
            dma((2,)), dma((4, CHUNKS)), dma((4, CHUNKS)),
            dma((4, most)), dma((4, most)),
        ],
        compiler_params=pltpu.CompilerParams(
            collective_id=0, has_side_effects=True, vmem_limit_bytes=40 << 20
        ),
        name="pair_gradients",
    )(image, text, log_temp, bias)
    return grad_image, grad_text, total_cl, total_c


def solution(mesh):
    rows = P(("blk", "grp"), None)
    return jax.shard_map(
        functools.partial(local, mesh.shape["blk"], mesh.shape["grp"]),
        mesh=mesh,
        in_specs=(rows, rows, P(), P()),
        out_specs=(rows, rows, P(), P()),
        check_vma=False,
    )
```

time: 221 us -> 75.2 us (0.34)
  blocking collectives: 168 us -> 0 us
  Pallas kernels: 0 us -> 64.2 us
  starting transfers between devices: 17.7 us -> 0 us
  waiting for transfers between devices: 15.7 us -> 0 us
  matrix products: 6.27 us -> 0 us
  other arithmetic: 5.4 us -> 0 us
  local copies, waits for them, and re-layouts: 0.01 us -> 4.15 us
  between operations: 8.11 us -> 5.44 us
    psum x1 -> x0, blocking collectives: 168 us -> none  [local(): total_c, total_cl = lax.psum((sum_c, sum_cl), ('blk', 'grp'))]
    pallas_call x0 -> x1, Pallas kernels: none -> 64.2 us  [local(): pl.pallas_call(functools.partial(kernel, (blk_n, grp_n, float(rows * blk_...]
    ppermute x2 -> x0, starting transfers between devices: 17.7 us -> none  [passed_along(): return lax.ppermute(value, axis, pairs)]
    ppermute x2 -> x0, waiting for transfers between devices: 15.7 us -> none  [passed_along(): return lax.ppermute(value, axis, pairs)]
    dot_general x6 -> x0, matrix products: 6.27 us -> none  [the longest x2 3.27 us: first_dot(): lax.dot_general(left, right, (((0,), (0,)), ((), ())), preferred_element_...]
    unnamed x4 -> x6, local copies, waits for them, and re-layouts: 0.01 us -> 4.15 us
    div x2 -> x0, other arithmetic: 2.58 us -> none  [norm_back(): return (grad_unit - unit * inner) / length]
  transfers between devices with their start and end apart: 2 -> 0, of which waited for: 1 -> 0; matrix products, arithmetic and copies ran while one was open for 2% -> 0% of each run, Pallas kernels for 0% -> 0%
where the time goes in v1:
time: 75.2 us; the launch traced here: 73.8 us
  Pallas kernels  64.2 us (85%)
  between operations  5.44 us (7%)
  local copies, waits for them, and re-layouts  4.15 us (6%)
    pallas_call x1, Pallas kernels, local(): pl.pallas_call(functools.partial(kernel, (blk_n, grp_n, float(rows * blk_...  64.2 us
    unnamed x6, local copies, waits for them, and re-layouts  4.15 us

profile of v1, /device:TPU:1, one launch (start us, length us, event | category | flops | bytes accessed | tf_op | source)
XLA Modules:
  0.0 73.8 jit_solution(5972983217308322981)
XLA Ops:
  1.9 0.0 copy-start
  1.9 1.1 %copy-done = bf16[256,1152]{1,0:T(8,128)(2,1)S(1)} copy-done((bf16[256,1152]{1,0:T(8,128)(2,1)S(1)}, bf16[256,1152]{1,0:T(8,128)(2,1)}, u32[]{:S(2)}) %copy-start) | copy-done | bytes 589848
  3.0 0.0 copy-start.1
  3.0 1.1 %copy-done.1 = bf16[256,1152]{1,0:T(8,128)(2,1)S(1)} copy-done((bf16[256,1152]{1,0:T(8,128)(2,1)S(1)}, bf16[256,1152]{1,0:T(8,128)(2,1)}, u32[]{:S(2)}) %copy-start.1) | copy-done | bytes 589848
  4.1 64.2 %pair_gradients.1 = (f32[256,1152]{1,0:T(8,128)S(1)}, f32[256,1152]{1,0:T(8,128)S(1)}, f32[1]{0:T(128)}, f32[1]{0:T(128)}) custom-call(bf16[256,1152]{1,0:T(8,128)(2,1)S(1)} %copy-done, bf16[256,1152]{1,0:T(8,128)(2,1)S(1)} %copy-done.1, f32[1]{0:T(128)S(6)} %copy.12.log_temp, f32[1]{0:T(128)S(6)} %copy.13.bias), custom_call_target="tpu_custom_call" | custom-call | tf_op jit(solution)/shard_map/pair_gradients/pallas_call | solution.py:241
  68.3 1.0 %copy.14 = f32[256,1152]{1,0:T(8,128)} copy(f32[256,1152]{1,0:T(8,128)S(1)} %get-tuple-element.8) | data formatting | bytes 2359296
  69.3 1.0 %copy.15 = f32[256,1152]{1,0:T(8,128)} copy(f32[256,1152]{1,0:T(8,128)S(1)} %get-tuple-element.9) | data formatting | bytes 2359296
Async XLA Ops:
  1.9 1.1 %copy-start = (bf16[256,1152]{1,0:T(8,128)(2,1)S(1)}, bf16[256,1152]{1,0:T(8,128)(2,1)}, u32[]{:S(2)}) copy-start(bf16[256,1152]{1,0:T(8,128)(2,1)} %img_in.1) | copy-start | bytes 1769476
  3.0 1.1 %copy-start.1 = (bf16[256,1152]{1,0:T(8,128)(2,1)S(1)}, bf16[256,1152]{1,0:T(8,128)(2,1)}, u32[]{:S(2)}) copy-start(bf16[256,1152]{1,0:T(8,128)(2,1)} %txt_in.1) | copy-start | bytes 1769476

commit v2 on v1

--- a/solution.py
+++ b/solution.py
@@ -10,7 +10,8 @@
 MESH = pl.DeviceIdType.MESH
 Y_HI, Y_LO, CORES = 4, 2, 2
 CHUNKS = 8
-HOLD = 5
+PARTS = 4
+TURNS = 3
 
 
 def row_dot(left, right):
@@ -34,12 +35,13 @@
 
 
 def kernel(
-    sizes, img_in, txt_in, log_temp, bias, gi_out, gt_out, cl_out, c_out,
+    sizes, img_in, txt_in, log_temp, bias, gi_out, gt_out, sum_out,
     img_raw, txt_raw, img_half, txt_half, img_inv, txt_inv,
     mid_txt, mid_img, end_txt, end_img, acc_txt, acc_img, sums,
-    part, load_sem, send_sem, recv_sem, sum_send, sum_recv,
+    part, climb, total, load_sem, send_sem, recv_sem, sum_send, sum_recv, climb_sem, drop_sem,
+    here_sem, base_sem, round_sem,
 ):
-    blk_n, grp_n, total_pairs = sizes
+    blk_n, grp_n = sizes
     x_n, z_n = blk_n // Y_HI, grp_n // (Y_LO * CORES)
     rows = img_raw.shape[0]
     step = rows // CHUNKS
@@ -67,11 +69,21 @@
     first = (first_blk, other)
     second = (lax.rem(first_blk + 1, blk_n), other)
 
+    base = z == 0
+
+    def along(k):
+        return at(x, lax.rem(y + k, Y_HI * Y_LO), z, core)
+
+    def across(k):
+        return at(lax.rem(x + k, x_n), y, z, core)
+
+    def twin(k):
+        return at(x, y, z, lax.rem(core + k, CORES))
+
     levels = (
-        (CORES, core, lambda k: at(x, y, z, k)),
-        (z_n, z, lambda k: at(x, y, k, core)),
-        (x_n, x, lambda k: at(k, y, z, core)),
-        (Y_HI * Y_LO, y, lambda k: at(x, k, z, core)),
+        (Y_HI * Y_LO, y, along),
+        (CORES, core, twin),
+        (x_n, x, across),
     )
 
     loads = [
@@ -82,17 +94,34 @@
         load.start()
 
     barrier = pltpu.get_barrier_semaphore()
-    greeted = 0
+
+    def greet(device):
+        pl.semaphore_signal(barrier, inc=1, device_id=device, device_id_type=MESH)
+
     for device in (meet_next, meet_prev, first, second):
-        pl.semaphore_signal(barrier, inc=1, device_id=device, device_id_type=MESH)
-        greeted += 1
-    for count, mine, place in levels:
-        for k in range(1, count):
-            pl.semaphore_signal(
-                barrier, inc=1, device_id=place(lax.rem(mine + k, count)),
-                device_id_type=MESH,
-            )
-            greeted += 1
+        greet(device)
+
+    @pl.when(z < z_n - 1)
+    def _():
+        greet(at(x, y, z + 1, core))
+
+    beside = (across(1), across(x_n - 1), along(1), along(Y_HI * Y_LO - 1))
+
+    @pl.when(base)
+    def _():
+        greet(beside[0])
+        greet(beside[1])
+        for k in range(1, CORES):
+            greet(twin(k))
+
+    greeted = 4 + (z > 0).astype(jnp.int32) + base.astype(jnp.int32) * (1 + CORES)
+
+    def signal(sem, device):
+        pl.semaphore_signal(sem, inc=1, device_id=device, device_id_type=MESH)
+
+    def tell(turn):
+        for device in beside:
+            signal(round_sem.at[turn], device)
 
     temp = jnp.exp(jnp.full((1, 1), log_temp[0], jnp.float32))
     shift = bias[0]
@@ -125,6 +154,14 @@
             pl.semaphore_wait(barrier, greeted)
         remote(txt_half, mid_txt, 0, c, meet_next).start()
         remote(img_half, mid_img, 1, c, meet_prev).start()
+
+    @pl.when(z > 1)
+    def _():
+        signal(here_sem, at(x, y, z - 1, core))
+
+    @pl.when(base)
+    def _():
+        tell(0)
 
     def coefs(sims, diagonal):
         scaled = temp * sims
@@ -144,6 +181,15 @@
     half = coef.T.astype(jnp.bfloat16)
     acc_txt[...] = plain_dot(half, img_half[...])
 
+    @pl.when(z > 1)
+    def _():
+        pl.semaphore_wait(base_sem, 1)
+
+    @pl.when(jnp.logical_and(z > 0, z < z_n - 1))
+    def _():
+        pl.semaphore_wait(here_sem, 1)
+        signal(base_sem, at(x, y, z + 1, core))
+
     def arrived(c):
         remote(txt_half, mid_txt, 0, c, meet_next).wait_recv()
         remote(img_half, mid_img, 1, c, meet_prev).wait_recv()
@@ -152,13 +198,8 @@
         remote(mid_txt, end_txt, 2, c, second).start()
         remote(mid_img, end_img, 3, c, first).start()
 
-    for c in range(HOLD):
+    for c in range(CHUNKS):
         arrived(c)
-    for c in range(HOLD):
-        send_on(c)
-    for c in range(HOLD, CHUNKS):
-        arrived(c)
-        send_on(c)
 
     coef, scaled = coefs(row_dot(mid_img[...], mid_txt[...]), False)
     part[0:8, :] = own_c + fold(coef)
@@ -172,35 +213,77 @@
         axis=0,
     )
 
-    def exchange(level, mine, place, k, count):
+    climb[0] = tile
+
+    def rise(k):
+        return pltpu.make_async_remote_copy(
+            src_ref=climb.at[0],
+            dst_ref=climb.at[k],
+            send_sem=climb_sem.at[0],
+            recv_sem=climb_sem.at[k],
+            device_id=at(x, y, 0, core),
+            device_id_type=MESH,
+        )
+
+    def drop(k):
+        return pltpu.make_async_remote_copy(
+            src_ref=total,
+            dst_ref=total,
+            send_sem=drop_sem.at[k],
+            recv_sem=drop_sem.at[0],
+            device_id=at(x, y, k, core),
+            device_id_type=MESH,
+        )
+
+    @pl.when(z > 0)
+    def _():
+        rise(z).start()
+        rise(z).wait_send()
+
+    for c in range(CHUNKS):
+        send_on(c)
+
+    @pl.when(base)
+    def _():
+        for turn in range(TURNS):
+            pl.semaphore_wait(round_sem.at[turn], 4)
+            if turn + 1 < TURNS:
+                tell(turn + 1)
+
+    def exchange(level, k):
+        count, mine, place = levels[level]
         return pltpu.make_async_remote_copy(
             src_ref=sums.at[level, mine],
             dst_ref=sums.at[level, mine],
             send_sem=sum_send.at[level, k],
             recv_sem=sum_recv.at[level, mine],
-            device_id=place(lax.rem(mine + k, count)),
+            device_id=place(k),
             device_id_type=MESH,
         )
 
-    for level, (count, mine, place) in enumerate(levels):
+    def incoming(level, k):
+        count, mine, place = levels[level]
+        source = lax.rem(mine + k, count)
+        return pltpu.make_async_remote_copy(
+            src_ref=sums.at[level, source],
+            dst_ref=sums.at[level, source],
+            send_sem=sum_send.at[level, k],
+            recv_sem=sum_recv.at[level, source],
+            device_id=place(k),
+            device_id_type=MESH,
+        )
+
+    def add_over(level, tile):
+        count, mine, _ = levels[level]
         sums[level, mine] = tile
         for k in range(1, count):
-            exchange(level, mine, place, k, count).start()
+            exchange(level, k).start()
         for k in range(1, count):
-            source = lax.rem(mine + k, count)
-            pltpu.make_async_remote_copy(
-                src_ref=sums.at[level, source],
-                dst_ref=sums.at[level, source],
-                send_sem=sum_send.at[level, k],
-                recv_sem=sum_recv.at[level, source],
-                device_id=place(source),
-                device_id_type=MESH,
-            ).wait_recv()
+            incoming(level, k).wait_recv()
         tile = sums[level, 0]
         for k in range(1, count):
             tile = tile + sums[level, k]
-    c_out[0] = jnp.sum(tile[0:1, :]) / total_pairs
-    cl_out[0] = jnp.sum(tile[1:2, :]) / total_pairs
+        return tile
 
     def finish(raw, half, inv, acc, visitors, out):
         coef, _ = coefs(row_dot(half[...], visitors[...]), False)
@@ -217,46 +300,107 @@
         remote(mid_img, end_img, 3, c, first).wait_recv()
     finish(txt_raw, txt_half, txt_inv, acc_txt, end_img, gt_out)
 
+    @pl.when(base)
+    def _():
+        for k in range(1, z_n):
+            rise(k).wait_recv()
+        tile = climb[0]
+        for k in range(1, z_n):
+            tile = tile + climb[k]
+        for level in range(len(levels)):
+            tile = add_over(level, tile)
+        total[...] = tile
+        for k in range(1, z_n):
+            drop(k).start()
+
     for c in range(CHUNKS):
         remote(txt_half, mid_txt, 0, c, meet_next).wait_send()
         remote(img_half, mid_img, 1, c, meet_prev).wait_send()
         remote(mid_txt, end_txt, 2, c, second).wait_send()
         remote(mid_img, end_img, 3, c, first).wait_send()
-    for level, (count, mine, place) in enumerate(levels):
-        for k in range(1, count):
-            exchange(level, mine, place, k, count).wait_send()
+
+    @pl.when(z > 0)
+    def _():
+        drop(z).wait_recv()
+
+    @pl.when(base)
+    def _():
+        for level, (count, _, _) in enumerate(levels):
+            for k in range(1, count):
+                exchange(level, k).wait_send()
+        for k in range(1, z_n):
+            drop(k).wait_send()
+
+    sum_out[...] = total[...]
+
+
+def leave(pairs, gi_in, gt_in, sum_in, gi_out, gt_out, cl_out, c_out, sem):
+    rows = gi_in.shape[0]
+    step = rows // PARTS
+    copies = []
+    for c in range(PARTS):
+        part = pl.ds(c * step, step)
+        for k, (src, dst) in enumerate(((gi_in, gi_out), (gt_in, gt_out))):
+            copies.append(
+                pltpu.make_async_copy(src.at[part, :], dst.at[part, :], sem.at[k, c])
+            )
+    for copy in copies:
+        copy.start()
+    c_out[0] = jnp.sum(sum_in[0:1, :]) / pairs
+    cl_out[0] = jnp.sum(sum_in[1:2, :]) / pairs
+    for copy in copies:
+        copy.wait()
 
 
 def local(blk_n, grp_n, image, text, log_temp, bias):
     rows, width = image.shape
-    most = max(CORES, grp_n // (Y_LO * CORES), blk_n // Y_HI, Y_HI * Y_LO)
+    z_n = grp_n // (Y_LO * CORES)
+    most = max(blk_n // Y_HI, Y_HI * Y_LO, CORES)
     wide = jax.ShapeDtypeStruct((rows, width), jnp.float32)
     one = jax.ShapeDtypeStruct((1,), jnp.float32)
+    slab = jax.ShapeDtypeStruct((8, 128), jnp.float32)
     half = pltpu.VMEM((rows, width), jnp.bfloat16)
     full = pltpu.VMEM((rows, width), jnp.float32)
     thin = pltpu.VMEM((rows, 1), jnp.float32)
-    vmem, smem = pl.BlockSpec(memory_space=pltpu.VMEM), pl.BlockSpec(memory_space=pltpu.SMEM)
-    hbm = pl.BlockSpec(memory_space=pl.ANY)
-    dma = pltpu.SemaphoreType.DMA
-    grad_image, grad_text, total_cl, total_c = pl.pallas_call(
-        functools.partial(kernel, (blk_n, grp_n, float(rows * blk_n * grp_n))),
-        out_shape=(wide, wide, one, one),
+    vmem = pl.BlockSpec(memory_space=pltpu.VMEM)
+    smem = pl.BlockSpec(memory_space=pltpu.SMEM)
+    hbm = pl.BlockSpec(memory_space=pltpu.HBM)
+    dma, plain = pltpu.SemaphoreType.DMA, pltpu.SemaphoreType.REGULAR
+    grads_and_sums = pl.pallas_call(
+        functools.partial(kernel, (blk_n, grp_n)),
+        out_shape=(wide, wide, slab),
         in_specs=[hbm, hbm, smem, smem],
-        out_specs=(vmem, vmem, smem, smem),
+        out_specs=(vmem, vmem, vmem),
         scratch_shapes=[
             half, half, half, half, thin, thin,
             half, half, half, half, full, full,
-            pltpu.VMEM((4, most, 8, 128), jnp.float32),
+            pltpu.VMEM((3, most, 8, 128), jnp.float32),
             pltpu.VMEM((16, 128), jnp.float32),
+            pltpu.VMEM((z_n, 8, 128), jnp.float32),
+            pltpu.VMEM((8, 128), jnp.float32),
             dma((2,)), dma((4, CHUNKS)), dma((4, CHUNKS)),
-            dma((4, most)), dma((4, most)),
+            dma((3, most)), dma((3, most)), dma((z_n,)), dma((z_n,)),
+            plain, plain, pltpu.SemaphoreType.REGULAR((TURNS,)),
         ],
         compiler_params=pltpu.CompilerParams(
             collective_id=0, has_side_effects=True, vmem_limit_bytes=40 << 20
         ),
         name="pair_gradients",
-    )(image, text, log_temp, bias)
-    return grad_image, grad_text, total_cl, total_c
+    )(
+        pltpu.with_memory_space_constraint(image, pltpu.HBM),
+        pltpu.with_memory_space_constraint(text, pltpu.HBM),
+        log_temp,
+        bias,
+    )
+    return pl.pallas_call(
+        functools.partial(leave, float(rows * blk_n * grp_n)),
+        out_shape=(wide, wide, one, one),
+        in_specs=[vmem, vmem, vmem],
+        out_specs=(hbm, hbm, smem, smem),
+        scratch_shapes=[dma((2, PARTS))],
+        compiler_params=pltpu.CompilerParams(vmem_limit_bytes=8 << 20),
+        name="leave",
+    )(*grads_and_sums)
 
 
 def solution(mesh):

time: 75.2 us -> 63.4 us (0.84); the launches traced: 73.8 us -> 63.2 us
  local copies, waits for them, and re-layouts: 4.15 us -> 0 us
  between operations: 5.44 us -> 1.93 us
  Pallas kernels: 64.2 us -> 61.3 us
    unnamed x6 -> x0, local copies, waits for them, and re-layouts: 4.15 us -> none
    pallas_call x1 -> x2, Pallas kernels: 64.2 us -> 61.3 us  [the longest x1 59.3 us: local(): pl.pallas_call(functools.partial(kernel, (blk_n, grp_n)), out_shape=(wide...]
where the time goes in v2:
time: 63.4 us; the launch traced here: 63.2 us
  Pallas kernels  61.3 us (97%)
  between operations  1.93 us (3%)
    pallas_call x1, Pallas kernels, local(): pl.pallas_call(functools.partial(kernel, (blk_n, grp_n)), out_shape=(wide...  59.3 us
    pallas_call x1, Pallas kernels, local(): pl.pallas_call(functools.partial(leave, float(rows * blk_n * grp_n)), out...  1.99 us

profile of v2, /device:TPU:1, one launch (start us, length us, event | category | flops | bytes accessed | tf_op | source)
XLA Modules:
  0.0 63.2 jit_solution(6562172227208546000)
XLA Ops:
  1.9 59.3 %pair_gradients.1 = (f32[256,1152]{1,0:T(8,128)S(1)}, f32[256,1152]{1,0:T(8,128)S(1)}, f32[8,128]{1,0:T(8,128)S(1)}) custom-call(bf16[256,1152]{1,0:T(8,128)(2,1)} %img_in.1, bf16[256,1152]{1,0:T(8,128)(2,1)} %txt_in.1, f32[1]{0:T(128)S(6)} %copy.8.log_temp, f32[1]{0:T(128)S(6)} %copy.9.bias), custom_call_target="tpu_custom_call" | custom-call | tf_op jit(solution)/shard_map/pair_gradients/pallas_call | solution.py:369
  61.2 2.0 %leave.1 = (f32[256,1152]{1,0:T(8,128)}, f32[256,1152]{1,0:T(8,128)}, f32[1]{0:T(128)}, f32[1]{0:T(128)}) custom-call(f32[256,1152]{1,0:T(8,128)S(1)} %get-tuple-element.7.gi_in, f32[256,1152]{1,0:T(8,128)S(1)} %get-tuple-element.8.gt_in, f32[8,128]{1,0:T(8,128)S(1)} %get-tuple-element.9.sum_in), custom_call_target="tpu_custom_call" | custom-call | tf_op jit(solution)/shard_map/leave/pallas_call | solution.py:395

commit v3 on v2

--- a/solution.py
+++ b/solution.py
@@ -38,7 +38,7 @@
     sizes, img_in, txt_in, log_temp, bias, gi_out, gt_out, sum_out,
     img_raw, txt_raw, img_half, txt_half, img_inv, txt_inv,
     mid_txt, mid_img, end_txt, end_img, acc_txt, acc_img, sums,
-    part, climb, total, load_sem, send_sem, recv_sem, sum_send, sum_recv, climb_sem, drop_sem,
+    part, climb, total, load_sem, send_sem, recv_sem, sum_send, sum_recv, rise_sem, climb_sem, drop_sem,
     here_sem, base_sem, round_sem,
 ):
     blk_n, grp_n = sizes
@@ -69,7 +69,9 @@
     first = (first_blk, other)
     second = (lax.rem(first_blk + 1, blk_n), other)
 
-    base = z == 0
+    root = min(1, z_n - 1)
+    base = z == root
+    slot = z * CORES + core
 
     def along(k):
         return at(x, lax.rem(y + k, Y_HI * Y_LO), z, core)
@@ -77,12 +79,11 @@
     def across(k):
         return at(lax.rem(x + k, x_n), y, z, core)
 
-    def twin(k):
-        return at(x, y, z, lax.rem(core + k, CORES))
+    def rooted(k):
+        return at(x, y, root, lax.rem(core + k, CORES))
 
     levels = (
         (Y_HI * Y_LO, y, along),
-        (CORES, core, twin),
         (x_n, x, across),
     )
 
@@ -101,7 +102,7 @@
     for device in (meet_next, meet_prev, first, second):
         greet(device)
 
-    @pl.when(z < z_n - 1)
+    @pl.when(jnp.logical_and(z >= root, z < z_n - 1))
     def _():
         greet(at(x, y, z + 1, core))
 
@@ -112,9 +113,11 @@
         greet(beside[0])
         greet(beside[1])
         for k in range(1, CORES):
-            greet(twin(k))
-
-    greeted = 4 + (z > 0).astype(jnp.int32) + base.astype(jnp.int32) * (1 + CORES)
+            greet(rooted(k))
+        for k in range(root):
+            greet(at(x, y, k, core))
+
+    greeted = 4 + jnp.where(base, 1 + CORES, 1)
 
     def signal(sem, device):
         pl.semaphore_signal(sem, inc=1, device_id=device, device_id_type=MESH)
@@ -155,9 +158,9 @@
         remote(txt_half, mid_txt, 0, c, meet_next).start()
         remote(img_half, mid_img, 1, c, meet_prev).start()
 
-    @pl.when(z > 1)
-    def _():
-        signal(here_sem, at(x, y, z - 1, core))
+    @pl.when(z != root)
+    def _():
+        signal(here_sem, at(x, y, jnp.where(z > root, z - 1, z + 1), core))
 
     @pl.when(base)
     def _():
@@ -181,13 +184,22 @@
     half = coef.T.astype(jnp.bfloat16)
     acc_txt[...] = plain_dot(half, img_half[...])
 
-    @pl.when(z > 1)
+    @pl.when(base)
+    def _():
+        pl.semaphore_wait(here_sem, root + min(1, z_n - 1 - root))
+        for k in range(root):
+            signal(base_sem, at(x, y, k, core))
+
+    @pl.when(z != root)
     def _():
         pl.semaphore_wait(base_sem, 1)
 
-    @pl.when(jnp.logical_and(z > 0, z < z_n - 1))
+    @pl.when(jnp.logical_and(z > root, z < z_n - 1))
     def _():
         pl.semaphore_wait(here_sem, 1)
+
+    @pl.when(jnp.logical_and(z >= root, z < z_n - 1))
+    def _():
         signal(base_sem, at(x, y, z + 1, core))
 
     def arrived(c):
@@ -213,15 +225,15 @@
         axis=0,
     )
 
-    climb[0] = tile
-
-    def rise(k):
+    climb[slot] = tile
+
+    def rise(k, place):
         return pltpu.make_async_remote_copy(
-            src_ref=climb.at[0],
-            dst_ref=climb.at[k],
-            send_sem=climb_sem.at[0],
-            recv_sem=climb_sem.at[k],
-            device_id=at(x, y, 0, core),
+            src_ref=climb.at[place],
+            dst_ref=climb.at[place],
+            send_sem=rise_sem.at[k],
+            recv_sem=climb_sem.at[place],
+            device_id=rooted(k),
             device_id_type=MESH,
         )
 
@@ -230,15 +242,24 @@
             src_ref=total,
             dst_ref=total,
             send_sem=drop_sem.at[k],
-            recv_sem=drop_sem.at[0],
+            recv_sem=drop_sem.at[z_n],
             device_id=at(x, y, k, core),
             device_id_type=MESH,
         )
 
-    @pl.when(z > 0)
-    def _():
-        rise(z).start()
-        rise(z).wait_send()
+    @pl.when(z != root)
+    def _():
+        for k in range(CORES):
+            rise(k, slot).start()
+        for k in range(CORES):
+            rise(k, slot).wait_send()
+
+    @pl.when(base)
+    def _():
+        for k in range(1, CORES):
+            rise(k, slot).start()
+        for k in range(1, CORES):
+            rise(k, slot).wait_send()
 
     for c in range(CHUNKS):
         send_on(c)
@@ -300,17 +321,22 @@
         remote(mid_img, end_img, 3, c, first).wait_recv()
     finish(txt_raw, txt_half, txt_inv, acc_txt, end_img, gt_out)
 
-    @pl.when(base)
-    def _():
-        for k in range(1, z_n):
-            rise(k).wait_recv()
+    others = [k for k in range(z_n) if k != root]
+
+    @pl.when(base)
+    def _():
+        for k in others:
+            for c in range(CORES):
+                rise(0, k * CORES + c).wait_recv()
+        for k in range(1, CORES):
+            rise(k, root * CORES + lax.rem(core + k, CORES)).wait_recv()
         tile = climb[0]
-        for k in range(1, z_n):
+        for k in range(1, z_n * CORES):
             tile = tile + climb[k]
         for level in range(len(levels)):
             tile = add_over(level, tile)
         total[...] = tile
-        for k in range(1, z_n):
+        for k in others:
             drop(k).start()
 
     for c in range(CHUNKS):
@@ -319,7 +345,7 @@
         remote(mid_txt, end_txt, 2, c, second).wait_send()
         remote(mid_img, end_img, 3, c, first).wait_send()
 
-    @pl.when(z > 0)
+    @pl.when(z != root)
     def _():
         drop(z).wait_recv()
 
@@ -328,7 +354,7 @@
         for level, (count, _, _) in enumerate(levels):
             for k in range(1, count):
                 exchange(level, k).wait_send()
-        for k in range(1, z_n):
+        for k in others:
             drop(k).wait_send()
 
     sum_out[...] = total[...]
@@ -374,12 +400,12 @@
         scratch_shapes=[
             half, half, half, half, thin, thin,
             half, half, half, half, full, full,
-            pltpu.VMEM((3, most, 8, 128), jnp.float32),
+            pltpu.VMEM((2, most, 8, 128), jnp.float32),
             pltpu.VMEM((16, 128), jnp.float32),
-            pltpu.VMEM((z_n, 8, 128), jnp.float32),
+            pltpu.VMEM((z_n * CORES, 8, 128), jnp.float32),
             pltpu.VMEM((8, 128), jnp.float32),
             dma((2,)), dma((4, CHUNKS)), dma((4, CHUNKS)),
-            dma((3, most)), dma((3, most)), dma((z_n,)), dma((z_n,)),
+            dma((2, most)), dma((2, most)), dma((CORES,)), dma((z_n * CORES,)), dma((z_n + 1,)),
             plain, plain, pltpu.SemaphoreType.REGULAR((TURNS,)),
         ],
         compiler_params=pltpu.CompilerParams(

time: 63.4 us -> 59.3 us (0.935)
  the two profiles are of different devices: /device:TPU:1 before, /device:TPU:2 now
where the time goes in v3:
time: 59.3 us; the launch traced here: 59.2 us
  Pallas kernels  57.2 us (96%)
  between operations  1.93 us (3%)
    pallas_call x1, Pallas kernels, local(): pl.pallas_call(functools.partial(kernel, (blk_n, grp_n)), out_shape=(wide...  55.2 us
    pallas_call x1, Pallas kernels, local(): pl.pallas_call(functools.partial(leave, float(rows * blk_n * grp_n)), out...  1.99 us

profile of v3, /device:TPU:2, one launch (start us, length us, event | category | flops | bytes accessed | tf_op | source)
XLA Modules:
  0.0 59.2 jit_solution(10710418058869711344)
XLA Ops:
  1.9 55.2 %pair_gradients.1 = (f32[256,1152]{1,0:T(8,128)S(1)}, f32[256,1152]{1,0:T(8,128)S(1)}, f32[8,128]{1,0:T(8,128)S(1)}) custom-call(bf16[256,1152]{1,0:T(8,128)(2,1)} %img_in.1, bf16[256,1152]{1,0:T(8,128)(2,1)} %txt_in.1, f32[1]{0:T(128)S(6)} %copy.8.log_temp, f32[1]{0:T(128)S(6)} %copy.9.bias), custom_call_target="tpu_custom_call" | custom-call | tf_op jit(solution)/shard_map/pair_gradients/pallas_call | solution.py:395
  57.2 2.0 %leave.1 = (f32[256,1152]{1,0:T(8,128)}, f32[256,1152]{1,0:T(8,128)}, f32[1]{0:T(128)}, f32[1]{0:T(128)}) custom-call(f32[256,1152]{1,0:T(8,128)S(1)} %get-tuple-element.7.gi_in, f32[256,1152]{1,0:T(8,128)S(1)} %get-tuple-element.8.gt_in, f32[8,128]{1,0:T(8,128)S(1)} %get-tuple-element.9.sum_in), custom_call_target="tpu_custom_call" | custom-call | tf_op jit(solution)/shard_map/leave/pallas_call | solution.py:421

commit v4 on v3

--- a/solution.py
+++ b/solution.py
@@ -69,18 +69,16 @@
     first = (first_blk, other)
     second = (lax.rem(first_blk + 1, blk_n), other)
 
-    root = min(1, z_n - 1)
+    root, chief = min(1, z_n - 1), CORES - 1
     base = z == root
-    slot = z * CORES + core
+    lead = jnp.logical_and(base, core == chief)
+    slot, lead_slot = z * CORES + core, root * CORES + chief
 
     def along(k):
         return at(x, lax.rem(y + k, Y_HI * Y_LO), z, core)
 
     def across(k):
         return at(lax.rem(x + k, x_n), y, z, core)
-
-    def rooted(k):
-        return at(x, y, root, lax.rem(core + k, CORES))
 
     levels = (
         (Y_HI * Y_LO, y, along),
@@ -108,16 +106,19 @@
 
     beside = (across(1), across(x_n - 1), along(1), along(Y_HI * Y_LO - 1))
 
-    @pl.when(base)
+    @pl.when(lead)
     def _():
         greet(beside[0])
         greet(beside[1])
+
+    @pl.when(base)
+    def _():
         for k in range(1, CORES):
-            greet(rooted(k))
+            greet(at(x, y, z, lax.rem(core + k, CORES)))
         for k in range(root):
             greet(at(x, y, k, core))
 
-    greeted = 4 + jnp.where(base, 1 + CORES, 1)
+    greeted = 4 + jnp.where(base, CORES - 1, 1) + jnp.where(lead, 2, 0)
 
     def signal(sem, device):
         pl.semaphore_signal(sem, inc=1, device_id=device, device_id_type=MESH)
@@ -162,7 +163,7 @@
     def _():
         signal(here_sem, at(x, y, jnp.where(z > root, z - 1, z + 1), core))
 
-    @pl.when(base)
+    @pl.when(lead)
     def _():
         tell(0)
 
@@ -227,13 +228,13 @@
 
     climb[slot] = tile
 
-    def rise(k, place):
+    def rise(place):
         return pltpu.make_async_remote_copy(
             src_ref=climb.at[place],
             dst_ref=climb.at[place],
-            send_sem=rise_sem.at[k],
+            send_sem=rise_sem,
             recv_sem=climb_sem.at[place],
-            device_id=rooted(k),
+            device_id=at(x, y, root, chief),
             device_id_type=MESH,
         )
 
@@ -242,29 +243,22 @@
             src_ref=total,
             dst_ref=total,
             send_sem=drop_sem.at[k],
-            recv_sem=drop_sem.at[z_n],
-            device_id=at(x, y, k, core),
+            recv_sem=drop_sem.at[z_n * CORES],
+            device_id=at(x, y, k // CORES, k % CORES),
             device_id_type=MESH,
         )
 
-    @pl.when(z != root)
-    def _():
-        for k in range(CORES):
-            rise(k, slot).start()
-        for k in range(CORES):
-            rise(k, slot).wait_send()
-
-    @pl.when(base)
-    def _():
-        for k in range(1, CORES):
-            rise(k, slot).start()
-        for k in range(1, CORES):
-            rise(k, slot).wait_send()
+    follows = jnp.logical_not(lead)
+
+    @pl.when(follows)
+    def _():
+        rise(slot).start()
+        rise(slot).wait_send()
 
     for c in range(CHUNKS):
         send_on(c)
 
-    @pl.when(base)
+    @pl.when(lead)
     def _():
         for turn in range(TURNS):
             pl.semaphore_wait(round_sem.at[turn], 4)
@@ -306,30 +300,12 @@
             tile = tile + sums[level, k]
         return tile
 
-    def finish(raw, half, inv, acc, visitors, out):
-        coef, _ = coefs(row_dot(half[...], visitors[...]), False)
-        grad = temp * (acc[...] + plain_dot(coef.astype(jnp.bfloat16), visitors[...]))
-        scale = inv[...]
-        unit = raw[...].astype(jnp.float32) * scale
-        inner = jnp.sum(unit * grad, axis=-1, keepdims=True)
-        out[...] = (grad - unit * inner) * scale
-
-    for c in range(CHUNKS):
-        remote(mid_txt, end_txt, 2, c, second).wait_recv()
-    finish(img_raw, img_half, img_inv, acc_img, end_txt, gi_out)
-    for c in range(CHUNKS):
-        remote(mid_img, end_img, 3, c, first).wait_recv()
-    finish(txt_raw, txt_half, txt_inv, acc_txt, end_img, gt_out)
-
-    others = [k for k in range(z_n) if k != root]
-
-    @pl.when(base)
+    others = [k for k in range(z_n * CORES) if k != lead_slot]
+
+    @pl.when(lead)
     def _():
         for k in others:
-            for c in range(CORES):
-                rise(0, k * CORES + c).wait_recv()
-        for k in range(1, CORES):
-            rise(k, root * CORES + lax.rem(core + k, CORES)).wait_recv()
+            rise(k).wait_recv()
         tile = climb[0]
         for k in range(1, z_n * CORES):
             tile = tile + climb[k]
@@ -339,17 +315,32 @@
         for k in others:
             drop(k).start()
 
+    def finish(raw, half, inv, acc, visitors, out):
+        coef, _ = coefs(row_dot(half[...], visitors[...]), False)
+        grad = temp * (acc[...] + plain_dot(coef.astype(jnp.bfloat16), visitors[...]))
+        scale = inv[...]
+        unit = raw[...].astype(jnp.float32) * scale
+        inner = jnp.sum(unit * grad, axis=-1, keepdims=True)
+        out[...] = (grad - unit * inner) * scale
+
+    for c in range(CHUNKS):
+        remote(mid_txt, end_txt, 2, c, second).wait_recv()
+    finish(img_raw, img_half, img_inv, acc_img, end_txt, gi_out)
+    for c in range(CHUNKS):
+        remote(mid_img, end_img, 3, c, first).wait_recv()
+    finish(txt_raw, txt_half, txt_inv, acc_txt, end_img, gt_out)
+
     for c in range(CHUNKS):
         remote(txt_half, mid_txt, 0, c, meet_next).wait_send()
         remote(img_half, mid_img, 1, c, meet_prev).wait_send()
         remote(mid_txt, end_txt, 2, c, second).wait_send()
         remote(mid_img, end_img, 3, c, first).wait_send()
 
-    @pl.when(z != root)
-    def _():
-        drop(z).wait_recv()
-
-    @pl.when(base)
+    @pl.when(follows)
+    def _():
+        drop(0).wait_recv()
+
+    @pl.when(lead)
     def _():
         for level, (count, _, _) in enumerate(levels):
             for k in range(1, count):
@@ -405,7 +396,7 @@
             pltpu.VMEM((z_n * CORES, 8, 128), jnp.float32),
             pltpu.VMEM((8, 128), jnp.float32),
             dma((2,)), dma((4, CHUNKS)), dma((4, CHUNKS)),
-            dma((2, most)), dma((2, most)), dma((CORES,)), dma((z_n * CORES,)), dma((z_n + 1,)),
+            dma((2, most)), dma((2, most)), dma, dma((z_n * CORES,)), dma((z_n * CORES + 1,)),
             plain, plain, pltpu.SemaphoreType.REGULAR((TURNS,)),
         ],
         compiler_params=pltpu.CompilerParams(

time: 59.3 us -> 56.8 us (0.958)
  the two profiles are of different devices: /device:TPU:2 before, /device:TPU:1 now
where the time goes in v4:
time: 56.8 us; the launch traced here: 56.6 us
  Pallas kernels  54.7 us (96%)
  between operations  1.93 us (3%)
    pallas_call x1, Pallas kernels, local(): pl.pallas_call(functools.partial(kernel, (blk_n, grp_n)), out_shape=(wide...  52.7 us
    pallas_call x1, Pallas kernels, local(): pl.pallas_call(functools.partial(leave, float(rows * blk_n * grp_n)), out...  1.99 us

profile of v4, /device:TPU:1, one launch (start us, length us, event | category | flops | bytes accessed | tf_op | source)
XLA Modules:
  0.0 56.6 jit_solution(3269426654462440485)
XLA Ops:
  1.9 52.7 %pair_gradients.1 = (f32[256,1152]{1,0:T(8,128)S(1)}, f32[256,1152]{1,0:T(8,128)S(1)}, f32[8,128]{1,0:T(8,128)S(1)}) custom-call(bf16[256,1152]{1,0:T(8,128)(2,1)} %img_in.1, bf16[256,1152]{1,0:T(8,128)(2,1)} %txt_in.1, f32[1]{0:T(128)S(6)} %copy.8.log_temp, f32[1]{0:T(128)S(6)} %copy.9.bias), custom_call_target="tpu_custom_call" | custom-call | tf_op jit(solution)/shard_map/pair_gradients/pallas_call | solution.py:386
  54.6 2.0 %leave.1 = (f32[256,1152]{1,0:T(8,128)}, f32[256,1152]{1,0:T(8,128)}, f32[1]{0:T(128)}, f32[1]{0:T(128)}) custom-call(f32[256,1152]{1,0:T(8,128)S(1)} %get-tuple-element.7.gi_in, f32[256,1152]{1,0:T(8,128)S(1)} %get-tuple-element.8.gt_in, f32[8,128]{1,0:T(8,128)S(1)} %get-tuple-element.9.sum_in), custom_call_target="tpu_custom_call" | custom-call | tf_op jit(solution)/shard_map/leave/pallas_call | solution.py:412
